TPU v7x, 32 devices: a whole 2x2x4 slice. The times are simulated.
32 devices in a mesh: gx: 4 (over z), gy: 8 (over y, x, core).
Axes of the slice: x: 2, y: 2, z: 4, core: 2. Of those that a mesh axis runs over, the one named last changes fastest.
Arguments:
- control: float32 [16, 1024, 512], P(None, 'gy', 'gx'), may hold values from -6 to 6
- scale_x: float32 [16, 512], replicated, may hold values from 2 to 384
- scale_y: float32 [16, 1024], P(None, 'gy'), may hold values from 2 to 384
- vertical_taps: float32 [5, 16], replicated, may hold values from 0.1 to 0.5
Outputs:
- increment: float32 [16, 1024, 512], P(None, 'gy', 'gx')
All inputs are finite; a program needn't handle non-finite values.
Results may differ from a plain program's by a relative error of at most 0.00016.
Values sent between devices are 32-bit elements; how exact they have to be, the bound alone decides.
A program may use at most 64 MiB of HBM per device.

v0:
```python
import functools

import jax
import jax.numpy as jnp
from jax import lax
from jax.experimental import pallas as pl
from jax.experimental.pallas import tpu as pltpu
from jax.sharding import PartitionSpec as P

MESH = pl.DeviceIdType.MESH
UNROLL = 8


def solvers(peers, levels):
    count = min(peers, levels)
    return count, levels // count


def sweep(streams, count, reverse):
    def body(t, carry):
        i = count - 1 - t if reverse else t
        new = []
        for (load, store, _), states in zip(streams, carry):
            pole, entry = load(i)
            keep = 1.0 - pole
            first = pole * states[0]
            if entry is not None:
                value, gain = entry
                first = first + (keep if gain is None else gain) * value
            second = pole * states[1] + keep * first
            third = pole * states[2] + keep * second
            fourth = pole * states[3] + keep * third
            store(i, fourth)
            new.append((first, second, third, fourth))
        return tuple(new)

    start = tuple(tuple(init) for _, _, init in streams)
    return lax.fori_loop(0, count, body, start, unroll=UNROLL)


def send(axis, peers, reach, src, dst, ssem, rsem):
    me = lax.axis_index(axis)
    for offset in range(1, peers):
        peer = lax.rem(me + offset, peers)

        def go(peer=peer):
            pltpu.make_async_remote_copy(
                src_ref=src(peer),
                dst_ref=dst(me),
                send_sem=ssem.at[peer],
                recv_sem=rsem.at[me],
                device_id={axis: peer},
                device_id_type=MESH,
            ).start()

        if reach == peers:
            go()
        else:
            pl.when(reach_of(reach, peer, me))(go)


def reach_of(reach, peer, me):
    count, who = reach if isinstance(reach, tuple) else (reach, "peer")
    return (peer if who == "peer" else me) < count


def settle(axis, peers, reach, src, dst, ssem, rsem, received):
    me = lax.axis_index(axis)
    for offset in range(1, peers):
        peer = lax.rem(me + offset, peers)

        def go(peer=peer):
            copy = pltpu.make_async_remote_copy(
                src_ref=src(peer),
                dst_ref=dst(peer),
                send_sem=ssem.at[peer],
                recv_sem=rsem.at[peer],
                device_id={axis: peer},
                device_id_type=MESH,
            )
            if received:
                copy.wait_recv()
            else:
                copy.wait_send()

        if reach == peers:
            go()
        else:
            pl.when(reach_of(reach, peer, me))(go)


def solve(links, closing, entering, peers, share):
    row = lax.broadcasted_iota(jnp.int32, (8, 128), 0)
    for s in range(share):
        rows = slice(8 * s, 8 * s + 8)
        low = jnp.zeros((8, 128), jnp.float32)
        lows, outs = [], []
        for k in range(peers):
            link = links[k, rows, :]
            out = closing[k, rows, :]
            if k > 0:
                for j in range(4):
                    out = out + link[:, j : j + 1] * low[j : j + 1, :]
            lows.append(low)
            outs.append(out)
            low = out
        high = jnp.zeros((8, 128), jnp.float32)
        for k in reversed(range(peers)):
            entering[k, rows, :] = jnp.where(row < 4, lows[k], high)
            out = outs[k]
            if k < peers - 1:
                link = links[k, rows, :]
                for j in range(4, 8):
                    out = out + link[:, j : j + 1] * high[j : j + 1, :]
            high = out


def correction(basis, entering, level, levels, length):
    wide = basis[pl.ds(level, length, stride=levels), :]
    lane = lax.broadcasted_iota(jnp.int32, wide.shape, 1)
    head = wide.astype(jnp.bfloat16).astype(jnp.float32)
    left = jnp.where(lane < 16, head, wide - head).astype(jnp.bfloat16)[:, :32]
    state = entering[8 * level : 8 * level + 8, :]
    state_head = state.astype(jnp.bfloat16).astype(jnp.float32)
    right = jnp.concatenate(
        [state_head, state - state_head, state_head, jnp.zeros_like(state)], axis=0
    ).astype(jnp.bfloat16)
    return jnp.dot(left, right, preferred_element_type=jnp.float32)


def kernel(
    nx, ny, control, scale_x, scale_y, out,
    vin, px, py, gy, xt, ubx, uby, z, yt,
    lx, ly, sx, sy, ex, ey, glx, gly, gsx, gsy, rx, ry,
    in_sem, xs, xr, ys, yr,
):
    levels, rows, cols = out.shape
    mx, my = lax.axis_index("gx"), lax.axis_index("gy")
    solve_x, share_x = solvers(nx, levels)
    solve_y, share_y = solvers(ny, levels)

    fetch = pltpu.make_async_copy(control, vin, in_sem)
    fetch.start()
    barrier = pltpu.get_barrier_semaphore()
    for axis, mine, peers in (("gx", mx, nx), ("gy", my, ny)):
        for offset in range(1, peers):
            pl.semaphore_signal(
                barrier, inc=1, device_id={axis: lax.rem(mine + offset, peers)}, device_id_type=MESH
            )

    own_x = scale_x[:, pl.ds(pl.multiple_of(mx * cols, cols), cols)]
    own_y = scale_y[...]
    pole_x = jnp.exp(-1.0 / own_x)
    pole_y = jnp.exp(-1.0 / own_y)
    gain_x = jnp.sqrt(8.0 * own_x)
    gain_y = (1.0 - pole_y) * jnp.sqrt(8.0 * own_y)
    for i in range(cols):
        px[i * levels : (i + 1) * levels, :] = jnp.broadcast_to(pole_x[:, i : i + 1], (levels, 128))
    for i in range(rows):
        py[i * levels : (i + 1) * levels, :] = jnp.broadcast_to(pole_y[:, i : i + 1], (levels, 128))
        gy[i * levels : (i + 1) * levels, :] = jnp.broadcast_to(gain_y[:, i : i + 1], (levels, 128))

    def at(i):
        return pl.ds(pl.multiple_of(i * levels, levels), levels)

    def put(ref):
        def store(i, value):
            ref[at(i), :] = value
        return store

    lane = lax.broadcasted_iota(jnp.int32, (levels, 128), 1) % 8
    fore = [(lane == k).astype(jnp.float32) for k in range(4)]
    back = [(lane == k + 4).astype(jnp.float32) for k in range(4)]
    blank = [jnp.zeros((levels, 128), jnp.float32)] * 4

    def keep_states(ref, first, states):
        for k in range(4):
            ref[pl.ds(first + k, levels, stride=8), :] = states[k]

    end_x, end_y = sweep(
        [
            (lambda i: (px[at(i), :], None), put(ubx), fore),
            (lambda i: (py[at(i), :], None), put(uby), fore),
        ],
        cols, False,
    )
    keep_states(lx, 0, end_x)
    keep_states(ly, 0, end_y)
    end_x, end_y = sweep(
        [
            (lambda i: (px[at(i), :], (ubx[at(i), :], None)), put(ubx), back),
            (lambda i: (py[at(i), :], (uby[at(i), :], None)), put(uby), back),
        ],
        cols, True,
    )
    keep_states(lx, 4, end_x)
    keep_states(ly, 4, end_y)

    pl.semaphore_wait(barrier, nx + ny - 2)

    def part(ref, share):
        return lambda peer: ref.at[pl.ds(pl.multiple_of(peer * share * 8, 8), share * 8), :]

    def slot(ref):
        return lambda peer: ref.at[peer]

    to_x = nx if solve_x == nx else (solve_x, "peer")
    at_x = nx if solve_x == nx else (solve_x, "me")
    to_y = ny if solve_y == ny else (solve_y, "peer")
    at_y = ny if solve_y == ny else (solve_y, "me")

    def plan(axis, peers, share, to, own, ssem, rsem, links, glinks, states, gstates, solved, entering):
        return [
            (axis, peers, to, own, part(links, share), slot(glinks), ssem.at[0], rsem.at[0]),
            (axis, peers, to, own, part(states, share), slot(gstates), ssem.at[1], rsem.at[1]),
            (axis, peers, own, to, slot(solved), part(entering, share), ssem.at[2], rsem.at[2]),
        ]

    plan_x = plan("gx", nx, share_x, to_x, at_x, xs, xr, lx, glx, sx, gsx, rx, ex)
    plan_y = plan("gy", ny, share_y, to_y, at_y, ys, yr, ly, gly, sy, gsy, ry, ey)

    def begin(p):
        axis, peers, sending, _, src, dst, ssem, rsem = p
        send(axis, peers, sending, src, dst, ssem, rsem)

    def landed(p):
        axis, peers, _, receiving, src, dst, ssem, rsem = p
        settle(axis, peers, receiving, src, dst, ssem, rsem, True)

    def left(p):
        axis, peers, sending, _, src, dst, ssem, rsem = p
        settle(axis, peers, sending, src, dst, ssem, rsem, False)

    begin(plan_x[0])
    begin(plan_y[0])

    fetch.wait()
    for l in range(levels):
        xt[pl.ds(l, cols, stride=levels), :] = (vin[l] * gain_x[l : l + 1, :]).T
    (end,) = sweep([(lambda i: (px[at(i), :], (xt[at(i), :], None)), put(xt), blank)], cols, False)
    keep_states(sx, 0, end)
    (end,) = sweep([(lambda i: (px[at(i), :], (xt[at(i), :], None)), put(xt), blank)], cols, True)
    keep_states(sx, 4, end)

    def entering_of(plan_, mine, peers, count, share, links, glinks, states, gstates, solved, entering):
        begin(plan_[1])

        def work():
            own = pl.ds(pl.multiple_of(mine * share * 8, 8), share * 8)
            glinks[mine] = links[own, :]
            gstates[mine] = states[own, :]

        def resolve():
            own = pl.ds(pl.multiple_of(mine * share * 8, 8), share * 8)
            solve(glinks, gstates, solved, peers, share)
            entering[own, :] = solved[mine]

        def run(f):
            if count == peers:
                f()
            else:
                pl.when(mine < count)(f)

        run(work)
        landed(plan_[0])
        landed(plan_[1])
        run(resolve)
        begin(plan_[2])
        landed(plan_[2])

    entering_of(plan_x, mx, nx, solve_x, share_x, lx, glx, sx, gsx, rx, ex)
    for l in range(levels):
        full = xt[pl.ds(l, cols, stride=levels), :] + correction(ubx, ex, l, levels, cols)
        z[l * rows : (l + 1) * rows, :] = full.T

    (end,) = sweep(
        [(lambda i: (py[at(i), :], (z[pl.ds(i, levels, stride=rows), :], gy[at(i), :])), put(yt), blank)],
        rows, False,
    )
    keep_states(sy, 0, end)
    (end,) = sweep([(lambda i: (py[at(i), :], (yt[at(i), :], None)), put(yt), blank)], rows, True)
    keep_states(sy, 4, end)

    entering_of(plan_y, my, ny, solve_y, share_y, ly, gly, sy, gsy, ry, ey)
    for l in range(levels):
        out[l] = yt[pl.ds(l, rows, stride=levels), :] + correction(uby, ey, l, levels, rows)

    for p in plan_x + plan_y:
        left(p)


def shards(control, scale_x, scale_y, vertical_taps):
    levels, rows, cols = control.shape
    nx, ny = lax.axis_size("gx"), lax.axis_size("gy")
    _, share_x = solvers(nx, levels)
    _, share_y = solvers(ny, levels)
    f32 = jnp.float32

    def flat(n):
        return pltpu.VMEM((n, 128), f32)

    values = pl.pallas_call(
        functools.partial(kernel, nx, ny),
        out_shape=jax.ShapeDtypeStruct((levels, rows, cols), f32),
        in_specs=[
            pl.BlockSpec(memory_space=pl.ANY),
            pl.BlockSpec(memory_space=pltpu.VMEM),
            pl.BlockSpec(memory_space=pltpu.VMEM),
        ],
        out_specs=pl.BlockSpec(memory_space=pltpu.VMEM),
        scratch_shapes=[
            pltpu.VMEM((levels, rows, cols), f32),
            flat(cols * levels), flat(rows * levels), flat(rows * levels),
            flat(cols * levels), flat(cols * levels), flat(rows * levels),
            flat(levels * rows), flat(rows * levels),
            flat(levels * 8), flat(levels * 8), flat(levels * 8), flat(levels * 8),
            flat(levels * 8), flat(levels * 8),
            pltpu.VMEM((nx, share_x * 8, 128), f32), pltpu.VMEM((ny, share_y * 8, 128), f32),
            pltpu.VMEM((nx, share_x * 8, 128), f32), pltpu.VMEM((ny, share_y * 8, 128), f32),
            pltpu.VMEM((nx, share_x * 8, 128), f32), pltpu.VMEM((ny, share_y * 8, 128), f32),
            pltpu.SemaphoreType.DMA,
            pltpu.SemaphoreType.DMA((3, nx)), pltpu.SemaphoreType.DMA((3, nx)),
            pltpu.SemaphoreType.DMA((3, ny)), pltpu.SemaphoreType.DMA((3, ny)),
        ],
        compiler_params=pltpu.CompilerParams(
            collective_id=0, has_side_effects=True, vmem_limit_bytes=32 * 1024 * 1024
        ),
    )(control, scale_x, scale_y)
    padded = jnp.pad(values, ((2, 2), (0, 0), (0, 0)))
    increment = jnp.zeros_like(values)
    for offset in range(5):
        increment = (
            increment + vertical_taps[offset][:, None, None] * padded[offset : offset + levels]
        )
    return increment


def solution(mesh):
    return jax.shard_map(
        shards,
        mesh=mesh,
        in_specs=(P(None, "gy", "gx"), P(), P(None, "gy"), P()),
        out_specs=P(None, "gy", "gx"),
        check_vma=False,
    )
```

profile of v0, /device:TPU:0, one launch (start us, length us, event | category | flops | bytes accessed | tf_op | source)
XLA Modules:
  0.0 31.9 jit_solution(15925114704039377558)
XLA Ops:
  0.0 0.9 %slice_bitcast_fusion.4 = (f32[16]{0:T(128)S(1)}, f32[16]{0:T(128)S(1)}, f32[16]{0:T(128)S(1)}, f32[16]{0:T(128)S(1)}, f32[16]{0:T(128)S(1)}) fusion(f32[5,16]{1,0:T(8,128)} %param.7), kind=kLoop, calls=%fused_computation.16 | loop fusion | bytes 640 | tf_op jit(solution)/shard_map/mul | solution.py:333
  0.9 0.0 copy-start
  0.9 1.2 %copy-done = f32[16,128,128]{2,1,0:T(8,128)S(1)} copy-done((f32[16,128,128]{2,1,0:T(8,128)S(1)}, f32[16,128,128]{2,1,0:T(8,128)}, u32[]{:S(2)}) %copy-start) | copy-done | bytes 1048600
  2.1 0.0 copy-start.1
  2.1 0.8 %copy-done.1 = f32[16,512]{1,0:T(8,128)S(1)} copy-done((f32[16,512]{1,0:T(8,128)S(1)}, f32[16,512]{1,0:T(8,128)}, u32[]{:S(2)}) %copy-start.1) | copy-done | bytes 32792
  2.9 0.0 copy-start.2
  2.9 0.7 %copy-done.2 = f32[16,128]{1,0:T(8,128)S(1)} copy-done((f32[16,128]{1,0:T(8,128)S(1)}, f32[16,128]{1,0:T(8,128)}, u32[]{:S(2)}) %copy-start.2) | copy-done | bytes 8216
  3.6 26.8 %shard_map.46 = f32[16,128,128]{2,1,0:T(8,128)S(1)} custom-call(f32[16,128,128]{2,1,0:T(8,128)S(1)} %copy-done, f32[16,512]{1,0:T(8,128)S(1)} %copy-done.1, f32[16,128]{1,0:T(8,128)S(1)} %copy-done.2), custom_call_target="tpu_custom_call" | custom-call | tf_op jit(solution)/shard_map/pallas_call | solution.py:302
  30.4 1.5 %fusion.4 = f32[16,128,128]{2,1,0:T(8,128)} fusion(f32[16,128,128]{2,1,0:T(8,128)S(1)} %shard_map.46, f32[16]{0:T(128)S(1)} %get-tuple-element.8, f32[16]{0:T(128)S(1)} %get-tuple-element.9, f32[16]{0:T(128)S(1)} %get-tuple-element.6, f32[16]{0:T(128)S(1)} %get-tuple-element.7, f32[16]{0:T(128)S(1)} %get-tuple-element.5), kind=kLoop, calls=%fused_computation.8 | loop fusion | flops 2359296 | bytes 2097472 | tf_op jit(solution)/shard_map/add | solution.py:333
Async XLA Ops:
  0.9 1.2 %copy-start = (f32[16,128,128]{2,1,0:T(8,128)S(1)}, f32[16,128,128]{2,1,0:T(8,128)}, u32[]{:S(2)}) copy-start(f32[16,128,128]{2,1,0:T(8,128)} %control.1) | copy-start | bytes 3145732
  2.1 0.8 %copy-start.1 = (f32[16,512]{1,0:T(8,128)S(1)}, f32[16,512]{1,0:T(8,128)}, u32[]{:S(2)}) copy-start(f32[16,512]{1,0:T(8,128)} %scale_x.1) | copy-start | bytes 98308
  2.9 0.7 %copy-start.2 = (f32[16,128]{1,0:T(8,128)S(1)}, f32[16,128]{1,0:T(8,128)}, u32[]{:S(2)}) copy-start(f32[16,128]{1,0:T(8,128)} %scale_y.1) | copy-start | bytes 24580
where the time goes:
time: 32.2 us; the launch traced here: 31.9 us
  Pallas kernels  26.8 us (83%)
  local copies, waits for them, and re-layouts  3.55 us (11%)
  other arithmetic  1.48 us (5%)
    pallas_call x1, Pallas kernels, shards(): pl.pallas_call(functools.partial(kernel, nx, ny), out_shape=jax.ShapeDtyp...  26.8 us
    unnamed x6, local copies, waits for them, and re-layouts  2.68 us
    add x1, other arithmetic, shards(): increment + vertical_taps[offset][:, None, None] * padded[offset:offset +...  1.48 us
    mul x1, local copies, waits for them, and re-layouts, shards(): vertical_taps[offset][:, None, None] * padded[offset:offset + levels]  0.87 us

commit v1 on v0

v1 whole, which is shorter than its diff:
```python
import functools

import jax
import jax.numpy as jnp
from jax import lax
from jax.experimental import pallas as pl
from jax.experimental.pallas import tpu as pltpu
from jax.sharding import PartitionSpec as P

MESH = pl.DeviceIdType.MESH
UNROLL = 8


def sweep(streams, count, reverse):
    def body(t, carry):
        i = count - 1 - t if reverse else t
        new = []
        for (load, store, _), states in zip(streams, carry):
            pole, entry = load(i)
            keep = 1.0 - pole
            first = pole * states[0]
            if entry is not None:
                value, gain = entry
                first = first + (keep if gain is None else gain) * value
            second = pole * states[1] + keep * first
            third = pole * states[2] + keep * second
            fourth = pole * states[3] + keep * third
            store(i, fourth)
            new.append((first, second, third, fourth))
        return tuple(new)

    start = tuple(tuple(init) for _, _, init in streams)
    return lax.fori_loop(0, count, body, start, unroll=UNROLL)


def each_peer(axis, peers, only, act):
    me = lax.axis_index(axis)
    for offset in range(1, peers):
        peer = lax.rem(me + offset, peers)
        if only is None:
            act(me, peer)
        else:
            pl.when(only(me, peer))(functools.partial(act, me, peer))


class Gather:
    def __init__(self, axis, peers, src, dst, ssem, rsem, downward=False):
        self.axis, self.peers, self.src, self.dst = axis, peers, src, dst
        self.ssem, self.rsem, self.downward = ssem, rsem, downward

    def copy(self, slot, peer):
        return pltpu.make_async_remote_copy(
            src_ref=self.src,
            dst_ref=self.dst.at[slot],
            send_sem=self.ssem.at[peer],
            recv_sem=self.rsem.at[slot],
            device_id={self.axis: peer},
            device_id_type=MESH,
        )

    def below(self):
        return (lambda me, peer: peer < me) if self.downward else None

    def above(self):
        return (lambda me, peer: peer > me) if self.downward else None

    def begin(self):
        each_peer(self.axis, self.peers, self.below(), lambda me, peer: self.copy(me, peer).start())

    def landed(self):
        each_peer(self.axis, self.peers, self.above(), lambda me, peer: self.copy(peer, peer).wait_recv())

    def left(self):
        each_peer(self.axis, self.peers, self.below(), lambda me, peer: self.copy(me, peer).wait_send())


def pack(links, lane):
    packed = links[0]
    for k in range(1, 8):
        packed = jnp.where(lane // 8 == k, links[k], packed)
    return packed


def solve(me, peers, links, fore, back, entering, levels):
    shape = (levels, 128)
    low = [jnp.zeros(shape, jnp.float32)] * 4
    mine = low
    outs = []

    def state(ref, k, n):
        return ref[k, n * levels : (n + 1) * levels, :]

    for k in range(peers):
        link = links[k]

        def weight(n, j):
            return jnp.broadcast_to(link[:, 8 * n + j : 8 * n + j + 1], shape)

        mine = [jnp.where(k == me, a, b) for a, b in zip(low, mine)]
        out = [state(back, k, n) for n in range(4)]
        nxt = [state(fore, k, n) for n in range(4)]
        if k > 0:
            for n in range(4):
                for j in range(4):
                    out[n] = out[n] + weight(4 + n, j) * low[j]
            run = [weight(n, 0) for n in range(4)]
            for n in range(4):
                for j in range(n + 1):
                    nxt[n] = nxt[n] + run[n - j] * low[j]
        outs.append(out)
        low = nxt
    high = [jnp.zeros(shape, jnp.float32)] * 4
    for k in range(peers - 1, 0, -1):
        link = links[k]
        run = [jnp.broadcast_to(link[:, 8 * (4 + n) + 4 : 8 * (4 + n) + 5], shape) for n in range(4)]
        new = list(outs[k])
        for n in range(4):
            for j in range(n + 1):
                new[n] = new[n] + run[n - j] * high[j]
        high = [jnp.where(k > me, a, b) for a, b in zip(new, high)]
    for n in range(4):
        entering[n * levels : (n + 1) * levels, :] = mine[n]
        entering[(4 + n) * levels : (5 + n) * levels, :] = high[n]


def right_side(entering, level, levels):
    state = entering[pl.ds(level, 8, stride=levels), :]
    first = state.astype(jnp.bfloat16).astype(jnp.float32)
    return jnp.concatenate(
        [first, state - first, first, jnp.zeros_like(state)], axis=0
    ).astype(jnp.bfloat16)


def split_parts(wide, group):
    first = wide.astype(jnp.bfloat16).astype(jnp.float32)
    return jnp.where(group < 16, first, wide - first).astype(jnp.bfloat16)


def kernel(
    nx, ny, control, scale_x, scale_y, out,
    vin, px, py, gy, xt, ubx, uby, z, yt, vx, vy,
    lx, ly, fx, bx, fy, by, ex, ey, glx, gly, gfx, gbx, gfy, gby,
    in_sem, xs, xr, ys, yr,
):
    levels, rows, cols = out.shape
    mx, my = lax.axis_index("gx"), lax.axis_index("gy")

    fetch = pltpu.make_async_copy(control, vin, in_sem)
    fetch.start()
    gbx[...] = jnp.zeros(gbx.shape, jnp.float32)
    gby[...] = jnp.zeros(gby.shape, jnp.float32)
    barrier = pltpu.get_barrier_semaphore()
    for axis, mine, peers in (("gx", mx, nx), ("gy", my, ny)):
        for offset in range(1, peers):
            pl.semaphore_signal(
                barrier, inc=1, device_id={axis: lax.rem(mine + offset, peers)}, device_id_type=MESH
            )

    own_x = scale_x[:, pl.ds(pl.multiple_of(mx * cols, cols), cols)]
    own_y = scale_y[...]
    pole_x = jnp.exp(-1.0 / own_x)
    pole_y = jnp.exp(-1.0 / own_y)
    gain_x = jnp.sqrt(8.0 * own_x)
    gain_y = (1.0 - pole_y) * jnp.sqrt(8.0 * own_y)
    for i in range(cols):
        px[i * levels : (i + 1) * levels, :] = jnp.broadcast_to(pole_x[:, i : i + 1], (levels, 128))
    for i in range(rows):
        py[i * levels : (i + 1) * levels, :] = jnp.broadcast_to(pole_y[:, i : i + 1], (levels, 128))
        gy[i * levels : (i + 1) * levels, :] = jnp.broadcast_to(gain_y[:, i : i + 1], (levels, 128))

    def at(i):
        return pl.ds(pl.multiple_of(i * levels, levels), levels)

    def put(ref):
        def store(i, value):
            ref[at(i), :] = value
        return store

    lane = lax.broadcasted_iota(jnp.int32, (levels, 128), 1)
    fore = [(lane % 8 == k).astype(jnp.float32) for k in range(4)]
    back = [(lane % 8 == k + 4).astype(jnp.float32) for k in range(4)]
    blank = [jnp.zeros((levels, 128), jnp.float32)] * 4

    def keep_states(ref, states):
        for k in range(4):
            ref[k * levels : (k + 1) * levels, :] = states[k]

    fore_x, fore_y = sweep(
        [
            (lambda i: (px[at(i), :], None), put(ubx), fore),
            (lambda i: (py[at(i), :], None), put(uby), fore),
        ],
        cols, False,
    )
    back_x, back_y = sweep(
        [
            (lambda i: (px[at(i), :], (ubx[at(i), :], None)), put(ubx), back),
            (lambda i: (py[at(i), :], (uby[at(i), :], None)), put(uby), back),
        ],
        cols, True,
    )
    lx[...] = pack(list(fore_x) + list(back_x), lane)
    ly[...] = pack(list(fore_y) + list(back_y), lane)

    pl.semaphore_wait(barrier, nx + ny - 2)

    links_x = Gather("gx", nx, lx, glx, xs.at[0], xr.at[0])
    fores_x = Gather("gx", nx, fx, gfx, xs.at[1], xr.at[1])
    backs_x = Gather("gx", nx, bx, gbx, xs.at[2], xr.at[2], True)
    links_y = Gather("gy", ny, ly, gly, ys.at[0], yr.at[0])
    fores_y = Gather("gy", ny, fy, gfy, ys.at[1], yr.at[1])
    backs_y = Gather("gy", ny, by, gby, ys.at[2], yr.at[2], True)
    links_x.begin()
    links_y.begin()

    fetch.wait()
    for l in range(levels):
        xt[pl.ds(l, cols, stride=levels), :] = (vin[l] * gain_x[l : l + 1, :]).T
    (end,) = sweep([(lambda i: (px[at(i), :], (xt[at(i), :], None)), put(xt), blank)], cols, False)
    keep_states(fx, end)
    fores_x.begin()
    (end,) = sweep([(lambda i: (px[at(i), :], (xt[at(i), :], None)), put(xt), blank)], cols, True)
    keep_states(bx, end)
    backs_x.begin()

    group = lax.broadcasted_iota(jnp.int32, (32, 128), 0)
    for l in range(levels):
        z[l * rows : (l + 1) * rows, :] = xt[pl.ds(l, cols, stride=levels), :].T
        wide = ubx[pl.ds(l, cols, stride=levels), :]
        vx[l * 32 : (l + 1) * 32, :] = split_parts(wide.T[:32, :], group)
    glx[mx] = lx[...]
    gfx[mx] = fx[...]
    gbx[mx] = bx[...]
    links_x.landed()
    fores_x.landed()
    backs_x.landed()
    solve(mx, nx, glx, gfx, gbx, ex, levels)
    for l in range(levels):
        z[l * rows : (l + 1) * rows, :] = z[l * rows : (l + 1) * rows, :] + lax.dot_general(
            right_side(ex, l, levels),
            vx[l * 32 : (l + 1) * 32, :],
            (((0,), (0,)), ((), ())),
            preferred_element_type=jnp.float32,
        )

    (end,) = sweep(
        [(lambda i: (py[at(i), :], (z[pl.ds(i, levels, stride=rows), :], gy[at(i), :])), put(yt), blank)],
        rows, False,
    )
    keep_states(fy, end)
    fores_y.begin()
    (end,) = sweep([(lambda i: (py[at(i), :], (yt[at(i), :], None)), put(yt), blank)], rows, True)
    keep_states(by, end)
    backs_y.begin()

    group = lax.broadcasted_iota(jnp.int32, (rows, 128), 1)
    for l in range(levels):
        vy[l * rows : (l + 1) * rows, :] = split_parts(uby[pl.ds(l, rows, stride=levels), :], group)
    gly[my] = ly[...]
    gfy[my] = fy[...]
    gby[my] = by[...]
    links_y.landed()
    fores_y.landed()
    backs_y.landed()
    solve(my, ny, gly, gfy, gby, ey, levels)
    for l in range(levels):
        out[l] = yt[pl.ds(l, rows, stride=levels), :] + jnp.dot(
            vy[l * rows : (l + 1) * rows, :][:, :32],
            right_side(ey, l, levels),
            preferred_element_type=jnp.float32,
        )

    for gather in (links_x, fores_x, backs_x, links_y, fores_y, backs_y):
        gather.left()


def band(taps, values, out, buffer, sems):
    levels = values.shape[0]
    copies = []
    for l in range(levels):
        total = None
        for d in range(5):
            if 0 <= l + d - 2 < levels:
                term = taps[d, l] * values[l + d - 2]
                total = term if total is None else total + term
        buffer[l] = total
        copies.append(pltpu.make_async_copy(buffer.at[l], out.at[l], sems.at[l]))
        copies[-1].start()
    for copy in copies:
        copy.wait()


def shards(control, scale_x, scale_y, vertical_taps):
    levels, rows, cols = control.shape
    nx, ny = lax.axis_size("gx"), lax.axis_size("gy")
    f32 = jnp.float32

    def flat(n, dtype=f32):
        return pltpu.VMEM((n, 128), dtype)

    def slots(n, height):
        return pltpu.VMEM((n, height, 128), f32)

    values = pl.pallas_call(
        functools.partial(kernel, nx, ny),
        out_shape=jax.ShapeDtypeStruct((levels, rows, cols), f32),
        in_specs=[
            pl.BlockSpec(memory_space=pltpu.HBM),
            pl.BlockSpec(memory_space=pltpu.VMEM),
            pl.BlockSpec(memory_space=pltpu.VMEM),
        ],
        out_specs=pl.BlockSpec(memory_space=pltpu.VMEM),
        scratch_shapes=[
            pltpu.VMEM((levels, rows, cols), f32),
            flat(cols * levels), flat(rows * levels), flat(rows * levels),
            flat(cols * levels), flat(cols * levels), flat(rows * levels),
            flat(levels * rows), flat(rows * levels),
            flat(levels * 32, jnp.bfloat16), flat(levels * rows, jnp.bfloat16),
            flat(levels), flat(levels),
            flat(levels * 4), flat(levels * 4), flat(levels * 4), flat(levels * 4),
            flat(levels * 8), flat(levels * 8),
            slots(nx, levels), slots(ny, levels),
            slots(nx, levels * 4), slots(nx, levels * 4),
            slots(ny, levels * 4), slots(ny, levels * 4),
            pltpu.SemaphoreType.DMA,
            pltpu.SemaphoreType.DMA((3, nx)), pltpu.SemaphoreType.DMA((3, nx)),
            pltpu.SemaphoreType.DMA((3, ny)), pltpu.SemaphoreType.DMA((3, ny)),
        ],
        compiler_params=pltpu.CompilerParams(
            collective_id=0, has_side_effects=True, vmem_limit_bytes=32 * 1024 * 1024
        ),
    )(control, scale_x, scale_y)
    return pl.pallas_call(
        band,
        out_shape=jax.ShapeDtypeStruct((levels, rows, cols), f32),
        in_specs=[
            pl.BlockSpec(memory_space=pltpu.SMEM),
            pl.BlockSpec(memory_space=pltpu.VMEM),
        ],
        out_specs=pl.BlockSpec(memory_space=pltpu.HBM),
        scratch_shapes=[
            pltpu.VMEM((levels, rows, cols), f32),
            pltpu.SemaphoreType.DMA((levels,)),
        ],
        compiler_params=pltpu.CompilerParams(vmem_limit_bytes=16 * 1024 * 1024),
    )(vertical_taps, values)


def solution(mesh):
    return jax.shard_map(
        shards,
        mesh=mesh,
        in_specs=(P(None, "gy", "gx"), P(), P(None, "gy"), P()),
        out_specs=P(None, "gy", "gx"),
        check_vma=False,
    )
```

time: 32.2 us -> 29.4 us (0.913)
  other arithmetic: 1.48 us -> 0 us
  local copies, waits for them, and re-layouts: 3.55 us -> 2.68 us
    pallas_call x1, Pallas kernels: 26.8 us -> 24.8 us  [shards(): pl.pallas_call(functools.partial(kernel, nx, ny), out_shape=jax.ShapeDtyp...]
    pallas_call x0 -> x1, Pallas kernels: none -> 1.7 us  [shards(): pl.pallas_call(band, out_shape=jax.ShapeDtypeStruct((levels, rows, cols),...]
    add x1 -> x0, other arithmetic: 1.48 us -> none  [shards(): increment + vertical_taps[offset][:, None, None] * padded[offset:offset +...]
    mul x1 -> x0, local copies, waits for them, and re-layouts: 0.87 us -> none  [shards(): vertical_taps[offset][:, None, None] * padded[offset:offset + levels]]
    unnamed x6 -> x8, local copies, waits for them, and re-layouts: 2.68 us -> 2.68 us
where the time goes in v1:
time: 29.4 us; the launch traced here: 29.2 us
  Pallas kernels  26.5 us (90%)
  local copies, waits for them, and re-layouts  2.68 us (9%)
    pallas_call x1, Pallas kernels, shards(): pl.pallas_call(functools.partial(kernel, nx, ny), out_shape=jax.ShapeDtyp...  24.8 us
    unnamed x8, local copies, waits for them, and re-layouts  2.68 us
    pallas_call x1, Pallas kernels, shards(): pl.pallas_call(band, out_shape=jax.ShapeDtypeStruct((levels, rows, cols),...  1.7 us

profile of v1, /device:TPU:0, one launch (start us, length us, event | category | flops | bytes accessed | tf_op | source)
XLA Modules:
  0.0 29.2 jit_solution(14350337772806545166)
XLA Ops:
  0.0 0.0 copy-start
  0.0 1.2 %copy-done = f32[16,128,128]{2,1,0:T(8,128)S(1)} copy-done((f32[16,128,128]{2,1,0:T(8,128)S(1)}, f32[16,128,128]{2,1,0:T(8,128)}, u32[]{:S(2)}) %copy-start) | copy-done | bytes 1048600
  1.2 0.0 copy-start.1
  1.2 0.8 %copy-done.1 = f32[16,512]{1,0:T(8,128)S(1)} copy-done((f32[16,512]{1,0:T(8,128)S(1)}, f32[16,512]{1,0:T(8,128)}, u32[]{:S(2)}) %copy-start.1) | copy-done | bytes 32792
  2.0 0.0 copy-start.2
  2.0 0.7 %copy-done.2 = f32[16,128]{1,0:T(8,128)S(1)} copy-done((f32[16,128]{1,0:T(8,128)S(1)}, f32[16,128]{1,0:T(8,128)}, u32[]{:S(2)}) %copy-start.2) | copy-done | bytes 8216
  2.7 0.0 copy-start.3
  2.7 24.8 %shard_map.46.values = f32[16,128,128]{2,1,0:T(8,128)S(1)} custom-call(f32[16,128,128]{2,1,0:T(8,128)S(1)} %copy-done, f32[16,512]{1,0:T(8,128)S(1)} %copy-done.1, f32[16,128]{1,0:T(8,128)S(1)} %copy-done.2), custom_call_target="tpu_custom_call" | custom-call | tf_op jit(solution)/shard_map/pallas_call | solution.py:304
  27.5 0.0 copy-done.3
  27.5 1.7 %shard_map.47 = f32[16,128,128]{2,1,0:T(8,128)} custom-call(f32[5,16]{1,0:T(8,128)S(1)} %copy-done.3, f32[16,128,128]{2,1,0:T(8,128)S(1)} %shard_map.46.values), custom_call_target="tpu_custom_call" | custom-call | tf_op jit(solution)/shard_map/pallas_call | solution.py:333
Async XLA Ops:
  0.0 1.2 %copy-start = (f32[16,128,128]{2,1,0:T(8,128)S(1)}, f32[16,128,128]{2,1,0:T(8,128)}, u32[]{:S(2)}) copy-start(f32[16,128,128]{2,1,0:T(8,128)} %control.1) | copy-start | bytes 3145732
  1.2 0.8 %copy-start.1 = (f32[16,512]{1,0:T(8,128)S(1)}, f32[16,512]{1,0:T(8,128)}, u32[]{:S(2)}) copy-start(f32[16,512]{1,0:T(8,128)} %scale_x.1) | copy-start | bytes 98308
  2.0 0.7 %copy-start.2 = (f32[16,128]{1,0:T(8,128)S(1)}, f32[16,128]{1,0:T(8,128)}, u32[]{:S(2)}) copy-start(f32[16,128]{1,0:T(8,128)} %scale_y.1) | copy-start | bytes 24580
  2.7 24.8 %copy-start.3 = (f32[5,16]{1,0:T(8,128)S(1)}, f32[5,16]{1,0:T(8,128)}, u32[]{:S(2)}) copy-start(f32[5,16]{1,0:T(8,128)} %taps.1) | copy-start | bytes 964

commit v2 on v1

--- a/solution.py
+++ b/solution.py
@@ -8,7 +8,7 @@
 from jax.sharding import PartitionSpec as P
 
 MESH = pl.DeviceIdType.MESH
-UNROLL = 8
+UNROLL = 128
 
 
 def sweep(streams, count, reverse):
@@ -44,9 +44,9 @@
 
 
 class Gather:
-    def __init__(self, axis, peers, src, dst, ssem, rsem, downward=False):
+    def __init__(self, axis, peers, src, dst, ssem, rsem, rule=None):
         self.axis, self.peers, self.src, self.dst = axis, peers, src, dst
-        self.ssem, self.rsem, self.downward = ssem, rsem, downward
+        self.ssem, self.rsem, self.rule = ssem, rsem, rule
 
     def copy(self, slot, peer):
         return pltpu.make_async_remote_copy(
@@ -59,10 +59,10 @@
         )
 
     def below(self):
-        return (lambda me, peer: peer < me) if self.downward else None
+        return self.rule
 
     def above(self):
-        return (lambda me, peer: peer > me) if self.downward else None
+        return None if self.rule is None else lambda me, peer: self.rule(peer, me)
 
     def begin(self):
         each_peer(self.axis, self.peers, self.below(), lambda me, peer: self.copy(me, peer).start())
@@ -98,11 +98,12 @@
 
         mine = [jnp.where(k == me, a, b) for a, b in zip(low, mine)]
         out = [state(back, k, n) for n in range(4)]
-        nxt = [state(fore, k, n) for n in range(4)]
+        nxt = [state(fore, k, n) for n in range(4)] if k < peers - 1 else None
         if k > 0:
             for n in range(4):
                 for j in range(4):
                     out[n] = out[n] + weight(4 + n, j) * low[j]
+        if 0 < k < peers - 1:
             run = [weight(n, 0) for n in range(4)]
             for n in range(4):
                 for j in range(n + 1):
@@ -205,11 +206,11 @@
     pl.semaphore_wait(barrier, nx + ny - 2)
 
     links_x = Gather("gx", nx, lx, glx, xs.at[0], xr.at[0])
-    fores_x = Gather("gx", nx, fx, gfx, xs.at[1], xr.at[1])
-    backs_x = Gather("gx", nx, bx, gbx, xs.at[2], xr.at[2], True)
+    fores_x = Gather("gx", nx, fx, gfx, xs.at[1], xr.at[1], lambda a, b: a < nx - 1)
+    backs_x = Gather("gx", nx, bx, gbx, xs.at[2], xr.at[2], lambda a, b: b < a)
     links_y = Gather("gy", ny, ly, gly, ys.at[0], yr.at[0])
-    fores_y = Gather("gy", ny, fy, gfy, ys.at[1], yr.at[1])
-    backs_y = Gather("gy", ny, by, gby, ys.at[2], yr.at[2], True)
+    fores_y = Gather("gy", ny, fy, gfy, ys.at[1], yr.at[1], lambda a, b: a < ny - 1)
+    backs_y = Gather("gy", ny, by, gby, ys.at[2], yr.at[2], lambda a, b: b < a)
     links_x.begin()
     links_y.begin()
 
@@ -327,7 +328,7 @@
             pltpu.SemaphoreType.DMA((3, ny)), pltpu.SemaphoreType.DMA((3, ny)),
         ],
         compiler_params=pltpu.CompilerParams(
-            collective_id=0, has_side_effects=True, vmem_limit_bytes=32 * 1024 * 1024
+            collective_id=0, has_side_effects=True, vmem_limit_bytes=52 * 1024 * 1024
         ),
     )(control, scale_x, scale_y)
     return pl.pallas_call(

time: 29.4 us -> 24.7 us (0.84)
  Pallas kernels: 26.5 us -> 23 us
  local copies, waits for them, and re-layouts: 2.68 us -> 1.46 us
    pallas_call x1, Pallas kernels: 24.8 us -> 21.3 us  [shards(): pl.pallas_call(functools.partial(kernel, nx, ny), out_shape=jax.ShapeDtyp...]
    unnamed x8 -> x6, local copies, waits for them, and re-layouts: 2.68 us -> 1.46 us
where the time goes in v2:
time: 24.7 us; the launch traced here: 24.5 us
  Pallas kernels  23 us (93%)
  local copies, waits for them, and re-layouts  1.46 us (6%)
    pallas_call x1, Pallas kernels, shards(): pl.pallas_call(functools.partial(kernel, nx, ny), out_shape=jax.ShapeDtyp...  21.3 us
    pallas_call x1, Pallas kernels, shards(): pl.pallas_call(band, out_shape=jax.ShapeDtypeStruct((levels, rows, cols),...  1.7 us
    unnamed x6, local copies, waits for them, and re-layouts  1.46 us

profile of v2, /device:TPU:0, one launch (start us, length us, event | category | flops | bytes accessed | tf_op | source)
XLA Modules:
  0.0 24.5 jit_solution(14770551015940597324)
XLA Ops:
  0.0 0.0 copy-start
  0.0 0.8 %copy-done = f32[16,512]{1,0:T(8,128)S(1)} copy-done((f32[16,512]{1,0:T(8,128)S(1)}, f32[16,512]{1,0:T(8,128)}, u32[]{:S(2)}) %copy-start) | copy-done | bytes 32792
  0.8 0.0 copy-start.1
  0.8 0.7 %copy-done.1 = f32[16,128]{1,0:T(8,128)S(1)} copy-done((f32[16,128]{1,0:T(8,128)S(1)}, f32[16,128]{1,0:T(8,128)}, u32[]{:S(2)}) %copy-start.1) | copy-done | bytes 8216
  1.5 0.0 copy-start.2
  1.5 21.3 %shard_map.46.values = f32[16,128,128]{2,1,0:T(8,128)S(1)} custom-call(f32[16,128,128]{2,1,0:T(8,128)} %control.1, f32[16,512]{1,0:T(8,128)S(1)} %copy-done, f32[16,128]{1,0:T(8,128)S(1)} %copy-done.1), custom_call_target="tpu_custom_call" | custom-call | tf_op jit(solution)/shard_map/pallas_call | solution.py:305
  22.8 0.0 copy-done.2
  22.8 1.7 %shard_map.47 = f32[16,128,128]{2,1,0:T(8,128)} custom-call(f32[5,16]{1,0:T(8,128)S(1)} %copy-done.2, f32[16,128,128]{2,1,0:T(8,128)S(1)} %shard_map.46.values), custom_call_target="tpu_custom_call" | custom-call | tf_op jit(solution)/shard_map/pallas_call | solution.py:334
Async XLA Ops:
  0.0 0.8 %copy-start = (f32[16,512]{1,0:T(8,128)S(1)}, f32[16,512]{1,0:T(8,128)}, u32[]{:S(2)}) copy-start(f32[16,512]{1,0:T(8,128)} %scale_x.1) | copy-start | bytes 98308
  0.8 0.7 %copy-start.1 = (f32[16,128]{1,0:T(8,128)S(1)}, f32[16,128]{1,0:T(8,128)}, u32[]{:S(2)}) copy-start(f32[16,128]{1,0:T(8,128)} %scale_y.1) | copy-start | bytes 24580
  1.5 21.3 %copy-start.2 = (f32[5,16]{1,0:T(8,128)S(1)}, f32[5,16]{1,0:T(8,128)}, u32[]{:S(2)}) copy-start(f32[5,16]{1,0:T(8,128)} %taps.1) | copy-start | bytes 964

commit v3 on v2

--- a/solution.py
+++ b/solution.py
@@ -165,10 +165,6 @@
     gain_y = (1.0 - pole_y) * jnp.sqrt(8.0 * own_y)
     for i in range(cols):
         px[i * levels : (i + 1) * levels, :] = jnp.broadcast_to(pole_x[:, i : i + 1], (levels, 128))
-    for i in range(rows):
-        py[i * levels : (i + 1) * levels, :] = jnp.broadcast_to(pole_y[:, i : i + 1], (levels, 128))
-        gy[i * levels : (i + 1) * levels, :] = jnp.broadcast_to(gain_y[:, i : i + 1], (levels, 128))
-
     def at(i):
         return pl.ds(pl.multiple_of(i * levels, levels), levels)
 
@@ -185,25 +181,6 @@
     def keep_states(ref, states):
         for k in range(4):
             ref[k * levels : (k + 1) * levels, :] = states[k]
-
-    fore_x, fore_y = sweep(
-        [
-            (lambda i: (px[at(i), :], None), put(ubx), fore),
-            (lambda i: (py[at(i), :], None), put(uby), fore),
-        ],
-        cols, False,
-    )
-    back_x, back_y = sweep(
-        [
-            (lambda i: (px[at(i), :], (ubx[at(i), :], None)), put(ubx), back),
-            (lambda i: (py[at(i), :], (uby[at(i), :], None)), put(uby), back),
-        ],
-        cols, True,
-    )
-    lx[...] = pack(list(fore_x) + list(back_x), lane)
-    ly[...] = pack(list(fore_y) + list(back_y), lane)
-
-    pl.semaphore_wait(barrier, nx + ny - 2)
 
     links_x = Gather("gx", nx, lx, glx, xs.at[0], xr.at[0])
     fores_x = Gather("gx", nx, fx, gfx, xs.at[1], xr.at[1], lambda a, b: a < nx - 1)
@@ -211,18 +188,40 @@
     links_y = Gather("gy", ny, ly, gly, ys.at[0], yr.at[0])
     fores_y = Gather("gy", ny, fy, gfy, ys.at[1], yr.at[1], lambda a, b: a < ny - 1)
     backs_y = Gather("gy", ny, by, gby, ys.at[2], yr.at[2], lambda a, b: b < a)
+
+    fetch.wait()
+    for l in range(levels):
+        xt[pl.ds(l, cols, stride=levels), :] = (vin[l] * gain_x[l : l + 1, :]).T
+    end, fore_x = sweep(
+        [
+            (lambda i: (px[at(i), :], (xt[at(i), :], None)), put(xt), blank),
+            (lambda i: (px[at(i), :], None), put(ubx), fore),
+        ],
+        cols, False,
+    )
+    keep_states(fx, end)
+    pl.semaphore_wait(barrier, nx + ny - 2)
+    fores_x.begin()
+    end, back_x = sweep(
+        [
+            (lambda i: (px[at(i), :], (xt[at(i), :], None)), put(xt), blank),
+            (lambda i: (px[at(i), :], (ubx[at(i), :], None)), put(ubx), back),
+        ],
+        cols, True,
+    )
+    keep_states(bx, end)
+    lx[...] = pack(list(fore_x) + list(back_x), lane)
     links_x.begin()
+    backs_x.begin()
+
+    for i in range(rows):
+        py[i * levels : (i + 1) * levels, :] = jnp.broadcast_to(pole_y[:, i : i + 1], (levels, 128))
+        gy[i * levels : (i + 1) * levels, :] = jnp.broadcast_to(gain_y[:, i : i + 1], (levels, 128))
+
+    (fore_y,) = sweep([(lambda i: (py[at(i), :], None), put(uby), fore)], rows, False)
+    (back_y,) = sweep([(lambda i: (py[at(i), :], (uby[at(i), :], None)), put(uby), back)], rows, True)
+    ly[...] = pack(list(fore_y) + list(back_y), lane)
     links_y.begin()
-
-    fetch.wait()
-    for l in range(levels):
-        xt[pl.ds(l, cols, stride=levels), :] = (vin[l] * gain_x[l : l + 1, :]).T
-    (end,) = sweep([(lambda i: (px[at(i), :], (xt[at(i), :], None)), put(xt), blank)], cols, False)
-    keep_states(fx, end)
-    fores_x.begin()
-    (end,) = sweep([(lambda i: (px[at(i), :], (xt[at(i), :], None)), put(xt), blank)], cols, True)
-    keep_states(bx, end)
-    backs_x.begin()
 
     group = lax.broadcasted_iota(jnp.int32, (32, 128), 0)
     for l in range(levels):

time: 24.7 us -> 24.3 us (0.984)
  Pallas kernels: 23 us -> 22.6 us
    pallas_call x1, Pallas kernels: 21.3 us -> 20.9 us  [shards(): pl.pallas_call(functools.partial(kernel, nx, ny), out_shape=jax.ShapeDtyp...]
where the time goes in v3:
time: 24.3 us; the launch traced here: 24.1 us
  Pallas kernels  22.6 us (93%)
  local copies, waits for them, and re-layouts  1.46 us (6%)
    pallas_call x1, Pallas kernels, shards(): pl.pallas_call(functools.partial(kernel, nx, ny), out_shape=jax.ShapeDtyp...  20.9 us
    pallas_call x1, Pallas kernels, shards(): pl.pallas_call(band, out_shape=jax.ShapeDtypeStruct((levels, rows, cols),...  1.7 us
    unnamed x6, local copies, waits for them, and re-layouts  1.46 us

profile of v3, /device:TPU:0, one launch (start us, length us, event | category | flops | bytes accessed | tf_op | source)
XLA Modules:
  0.0 24.1 jit_solution(862788801330085280)
XLA Ops:
  0.0 0.0 copy-start
  0.0 0.8 %copy-done = f32[16,512]{1,0:T(8,128)S(1)} copy-done((f32[16,512]{1,0:T(8,128)S(1)}, f32[16,512]{1,0:T(8,128)}, u32[]{:S(2)}) %copy-start) | copy-done | bytes 32792
  0.8 0.0 copy-start.1
  0.8 0.7 %copy-done.1 = f32[16,128]{1,0:T(8,128)S(1)} copy-done((f32[16,128]{1,0:T(8,128)S(1)}, f32[16,128]{1,0:T(8,128)}, u32[]{:S(2)}) %copy-start.1) | copy-done | bytes 8216
  1.5 0.0 copy-start.2
  1.5 20.9 %shard_map.46.values = f32[16,128,128]{2,1,0:T(8,128)S(1)} custom-call(f32[16,128,128]{2,1,0:T(8,128)} %control.1, f32[16,512]{1,0:T(8,128)S(1)} %copy-done, f32[16,128]{1,0:T(8,128)S(1)} %copy-done.1), custom_call_target="tpu_custom_call" | custom-call | tf_op jit(solution)/shard_map/pallas_call | solution.py:304
  22.4 0.0 copy-done.2
  22.4 1.7 %shard_map.47 = f32[16,128,128]{2,1,0:T(8,128)} custom-call(f32[5,16]{1,0:T(8,128)S(1)} %copy-done.2, f32[16,128,128]{2,1,0:T(8,128)S(1)} %shard_map.46.values), custom_call_target="tpu_custom_call" | custom-call | tf_op jit(solution)/shard_map/pallas_call | solution.py:333
Async XLA Ops:
  0.0 0.8 %copy-start = (f32[16,512]{1,0:T(8,128)S(1)}, f32[16,512]{1,0:T(8,128)}, u32[]{:S(2)}) copy-start(f32[16,512]{1,0:T(8,128)} %scale_x.1) | copy-start | bytes 98308
  0.8 0.7 %copy-start.1 = (f32[16,128]{1,0:T(8,128)S(1)}, f32[16,128]{1,0:T(8,128)}, u32[]{:S(2)}) copy-start(f32[16,128]{1,0:T(8,128)} %scale_y.1) | copy-start | bytes 24580
  1.5 20.9 %copy-start.2 = (f32[5,16]{1,0:T(8,128)S(1)}, f32[5,16]{1,0:T(8,128)}, u32[]{:S(2)}) copy-start(f32[5,16]{1,0:T(8,128)} %taps.1) | copy-start | bytes 964
